TPU v7x, 32 devices: a whole 2x2x4 slice. The times are simulated.
32 devices in a mesh: tm: 16 (over z, y, x), chan: 2 (over core).
Axes of the slice: x: 2, y: 2, z: 4, core: 2. Of those that a mesh axis runs over, the one named last changes fastest.
Arguments:
- strain: bfloat16 [128, 131072], P('chan', 'tm'), as said below
- fir_taps: float32 [128, 64], P('chan'), may hold values from -0.75 to 0.75
Outputs:
- factor: float32 [1024, 1024], P(('tm', 'chan'))
- whitened: bfloat16 [1024, 16384], P(None, ('tm', 'chan'))
Inputs may be any that keep to these rules, and one draw needn't show every extreme that they name: strain-rate samples of 128 channels.
All inputs are finite; a program needn't handle non-finite values.
Results may differ from a plain program's by a relative error of at most 0.001.
The roundings to bfloat16 on the way count: a program that leaves them out, or rounds other values in their place, can miss the bound.
Values may be sent and summed in bfloat16 or wider, within the bound.
A program may use at most 128 MiB of HBM per device.

v0:
```python
import jax
import jax.numpy as jnp
from jax import lax
from jax.sharding import PartitionSpec as P

LAGS = 8
TAPS = 64
STRIDE = 8


def shifted(value, axis, steps):
    count = lax.axis_size(axis)
    initial, last = (max(0, -steps), min(count, count - steps))
    return lax.ppermute(value, axis, [(source, source + steps) for source in range(initial, last)])


def decimate(extended, fir_taps, out_rows):
    channels = extended.shape[0]
    phases = jnp.transpose(extended.astype(jnp.float32).reshape(channels, -1, STRIDE), (0, 2, 1))
    running = jnp.zeros((channels, out_rows), jnp.float32)
    for j in range(TAPS // STRIDE):
        window = phases[:, :, j : j + out_rows]
        weights = fir_taps[:, j * STRIDE : (j + 1) * STRIDE]
        running = running + jnp.einsum(
            "csn,cs->cn", window, weights, precision=lax.Precision.HIGHEST
        )
    return running


def inner_gram(left_rows, right_rows):
    return lax.dot_general(
        left_rows, right_rows, (((1,), (1,)), ((), ())), preferred_element_type=jnp.float32
    )


def local(strain, fir_taps):
    samples = strain.shape[1]
    out_rows = samples // STRIDE
    rim_len = TAPS - STRIDE
    rim_raw = shifted(strain[:, :rim_len], "tm", -1)
    extended = jnp.concatenate([strain, rim_raw], axis=1)
    local_rows = decimate(extended, fir_taps, out_rows).astype(jnp.bfloat16)
    tail_rows = shifted(local_rows[:, : LAGS - 1], "tm", -1)
    decimated = jnp.concatenate([local_rows, tail_rows], axis=1)
    gathered = lax.all_gather(decimated, "chan", axis=0, tiled=True)
    row_count = out_rows // lax.axis_size("chan")
    first_col = lax.axis_index("chan") * row_count
    window = lax.dynamic_slice_in_dim(gathered, first_col, row_count + LAGS - 1, 1)
    hankel = jnp.concatenate([window[:, i : i + row_count] for i in range(LAGS)], axis=0)
    columns = hankel.shape[0]
    gram_full = lax.psum(inner_gram(hankel, hankel), ("tm", "chan"))
    devices_all = lax.axis_size(("tm", "chan"))
    covariance = gram_full / (row_count * devices_all)
    lower_factor = jnp.linalg.cholesky(covariance)
    factor_rows = columns // devices_all
    first_row = lax.axis_index(("tm", "chan")) * factor_rows
    factor_mine = lax.dynamic_slice_in_dim(lower_factor, first_row, factor_rows, 1).T
    whitened = jax.scipy.linalg.solve_triangular(
        lower_factor, hankel.astype(jnp.float32), lower=True
    )
    return (factor_mine, whitened.astype(jnp.bfloat16))


def solution(mesh):
    placed = (P("chan", "tm"), P("chan", None))
    return jax.shard_map(
        local,
        mesh=mesh,
        in_specs=placed,
        out_specs=(P(("tm", "chan"), None), P(None, ("tm", "chan"))),
        check_vma=False,
    )
```

profile of v0, /device:TPU:0, one launch (start us, length us, event | category | flops | bytes accessed | tf_op | source)
XLA Modules:
  0.0 586.8 jit_solution(7478276221011478313)
XLA Ops:
  10.4 4.1 collective-permute-done
  17.6 5.9 fusion.66
  23.5 4.4 copy.46
  27.9 4.3 copy.43
  32.1 4.3 copy.40
  36.4 3.3 copy.37
  39.8 4.4 copy.34
  44.2 4.3 copy.31
  48.5 4.3 copy.28
  52.8 2.7 copy.25
  55.5 2.3 fusion.75
  70.1 5.2 collective-permute-done.1
  78.4 3.3 fusion.76
  82.0 145.1 %all-reduce.3.cloned.1.call-done = f32[1024,1024]{0,1:T(8,128)} async-done(((f32[1024,1024]{0,1:T(8,128)}), f32[1024,1024]{0,1:T(8,128)}) %all-reduce.3.cloned.1.call-update) | async-done | bytes 4194320 | tf_op jit(solution)/shard_map/psum | solution.py:51
  227.0 5.0 broadcast_multiply_fusion
  232.0 5.5 copy.16
  237.6 4.4 fusion
  244.0 11.7 %cholesky.223 = f32[128,128]{1,0:T(8,128)S(1)} custom-call(f32[128,128]{1,0:T(8,128)S(1)} %cholesky.580), custom_call_target="Cholesky" | custom-call | tf_op jit(solution)/shard_map/jit(cholesky)/cholesky | solution.py:54
  255.7 9.8 %custom-call.63 = f32[1,128,128]{1,2,0:T(8,128)S(1)} custom-call(f32[1,128,128]{2,1,0:T(8,128)S(1)} %get-tuple-element.72), custom_call_target="InvertDiagBlocksLowerTriangular" | custom-call | tf_op jit(solution)/shard_map/jit(cholesky)/cholesky | solution.py:54
  267.2 2.7 convolution_subtract_fusion
  271.0 12.1 %cholesky.244 = f32[128,128]{1,0:T(8,128)S(1)} custom-call(f32[128,128]{1,0:T(8,128)S(1)} %cholesky.584), custom_call_target="Cholesky" | custom-call | tf_op jit(solution)/shard_map/jit(cholesky)/cholesky | solution.py:54
  283.1 2.5 cholesky.255
  287.1 9.8 %custom-call.64 = f32[1,128,128]{1,2,0:T(8,128)S(1)} custom-call(f32[1,128,128]{2,1,0:T(8,128)S(1)} %get-tuple-element.69), custom_call_target="InvertDiagBlocksLowerTriangular" | custom-call | tf_op jit(solution)/shard_map/jit(cholesky)/cholesky | solution.py:54
  300.3 11.7 %cholesky.468 = f32[128,128]{1,0:T(8,128)S(1)} custom-call(f32[128,128]{1,0:T(8,128)S(1)} %cholesky.589), custom_call_target="Cholesky" | custom-call | tf_op jit(solution)/shard_map/jit(cholesky)/cholesky | solution.py:54
  312.7 9.8 %custom-call.65 = f32[1,128,128]{1,2,0:T(8,128)S(1)} custom-call(f32[1,128,128]{2,1,0:T(8,128)S(1)} %get-tuple-element.66), custom_call_target="InvertDiagBlocksLowerTriangular" | custom-call | tf_op jit(solution)/shard_map/jit(cholesky)/cholesky | solution.py:54
  323.6 2.3 convolution_subtract_fusion.2
  326.0 11.9 %cholesky.487 = f32[128,128]{1,0:T(8,128)S(1)} custom-call(f32[128,128]{1,0:T(8,128)S(1)} %cholesky.594), custom_call_target="Cholesky" | custom-call | tf_op jit(solution)/shard_map/jit(cholesky)/cholesky | solution.py:54
  338.5 9.8 %custom-call.66 = f32[1,128,128]{1,2,0:T(8,128)S(1)} custom-call(f32[1,128,128]{2,1,0:T(8,128)S(1)} %get-tuple-element.63), custom_call_target="InvertDiagBlocksLowerTriangular" | custom-call | tf_op jit(solution)/shard_map/jit(cholesky)/cholesky | solution.py:54
  349.4 2.3 convolution_subtract_fusion.10
  351.8 11.7 %cholesky.506 = f32[128,128]{1,0:T(8,128)S(1)} custom-call(f32[128,128]{1,0:T(8,128)S(1)} %cholesky.599), custom_call_target="Cholesky" | custom-call | tf_op jit(solution)/shard_map/jit(cholesky)/cholesky | solution.py:54
  364.1 10.0 %custom-call.67 = f32[1,128,128]{1,2,0:T(8,128)S(1)} custom-call(f32[1,128,128]{2,1,0:T(8,128)S(1)} %get-tuple-element.60), custom_call_target="InvertDiagBlocksLowerTriangular" | custom-call | tf_op jit(solution)/shard_map/jit(cholesky)/cholesky | solution.py:54
  375.2 2.3 convolution_subtract_fusion.11
  377.5 11.7 %cholesky.526 = f32[128,128]{1,0:T(8,128)S(1)} custom-call(f32[128,128]{1,0:T(8,128)S(1)} %cholesky.604), custom_call_target="Cholesky" | custom-call | tf_op jit(solution)/shard_map/jit(cholesky)/cholesky | solution.py:54
  389.8 9.8 %custom-call.68 = f32[1,128,128]{1,2,0:T(8,128)S(1)} custom-call(f32[1,128,128]{2,1,0:T(8,128)S(1)} %get-tuple-element.57), custom_call_target="InvertDiagBlocksLowerTriangular" | custom-call | tf_op jit(solution)/shard_map/jit(cholesky)/cholesky | solution.py:54
  402.6 12.1 %cholesky.546 = f32[128,128]{1,0:T(8,128)S(1)} custom-call(f32[128,128]{1,0:T(8,128)S(1)} %cholesky.609), custom_call_target="Cholesky" | custom-call | tf_op jit(solution)/shard_map/jit(cholesky)/cholesky | solution.py:54
  415.3 9.8 %custom-call.69 = f32[1,128,128]{1,2,0:T(8,128)S(1)} custom-call(f32[1,128,128]{2,1,0:T(8,128)S(1)} %get-tuple-element.54), custom_call_target="InvertDiagBlocksLowerTriangular" | custom-call | tf_op jit(solution)/shard_map/jit(cholesky)/cholesky | solution.py:54
  427.8 11.7 %cholesky.564 = f32[128,128]{1,0:T(8,128)S(1)} custom-call(f32[128,128]{1,0:T(8,128)S(1)} %convolution_subtract_fusion.13), custom_call_target="Cholesky" | custom-call | tf_op jit(solution)/shard_map/jit(cholesky)/cholesky | solution.py:54
  449.7 4.8 fusion.1
  455.6 27.7 %while.1 = (s32[]{:T(128)}, f32[1024,1024]{1,0:T(8,128)}, s32[8,2]{0,1:T(2,128)S(1)}, f32[8,128,128]{2,1,0:T(8,128)}, s32[]{:T(128)}) while((s32[]{:T(128)}, f32[1024,1024]{1,0:T(8,128)}, s32[8,2]{0,1:T(2,128)S(1)}, f32[8,128,128]{2,1,0:T(8,128)}, s32[]{:T(128)}) %tuple.73), condition=%wide.while_cond, body=%wide.while_body.sunk | while | flops 2 | bytes 132205 | solution.py:58
  456.2 2.9 bitcast_dynamic-update-slice_fusion.2
  459.7 2.9 bitcast_dynamic-update-slice_fusion.2
  463.1 2.9 bitcast_dynamic-update-slice_fusion.2
  466.6 2.9 bitcast_dynamic-update-slice_fusion.2
  470.1 2.9 bitcast_dynamic-update-slice_fusion.2
  473.6 2.9 bitcast_dynamic-update-slice_fusion.2
  477.0 2.9 bitcast_dynamic-update-slice_fusion.2
  480.5 2.8 bitcast_dynamic-update-slice_fusion.2
  483.3 79.6 %custom-call.70 = f32[8,128,128]{1,2,0:T(8,128)S(1)} custom-call(f32[8,128,128]{2,1,0:T(8,128)} %get-tuple-element.9), custom_call_target="InvertDiagBlocksLowerTriangular" | custom-call | tf_op jit(solution)/shard_map/jit(_solve_triangular)/triangular_solve | solution.py:58
  (121 shorter events, 71.4 us)
Async XLA Ops:
  7.2 219.9 %all-reduce.3.cloned.1.call-start = ((), (), s32[]{:S(2)}) async-start(), calls=%async_computation | async-start | bytes 8388608 | tf_op jit(solution)/shard_map/psum | solution.py:51
  7.9 6.5 %collective-permute-start = (bf16[64,56]{1,0:T(8,128)(2,1)S(1)}, bf16[64,56]{1,0:T(8,128)(2,1)S(1)}, u32[]{:S(2)}, u32[]{:S(2)}) collective-permute-start(bf16[64,56]{1,0:T(8,128)(2,1)S(1)} %slice.324), channel_id=1, source_target_pairs={{2,0},{4,2},{6,4},{8,6},{10,8},{12,10},{14,12},{16,14},{18,16},{20... | collective-permute-start | bytes 21512 | tf_op jit(solution)/shard_map/ppermute | solution.py:14
  23.5 12.9 %copy-start.2 = (bf16[64,8,1024]{0,1,2:T(8,128)(2,1)S(1)}, bf16[64,8,1024]{0,1,2:T(8,128)(2,1)}, u32[]{:S(2)}) copy-start(bf16[64,8,1024]{0,1,2:T(8,128)(2,1)} %get-tuple-element.30) | copy-start | bytes 3145732
  39.8 13.0 %copy-start.1 = (bf16[64,8,1024]{0,1,2:T(8,128)(2,1)S(1)}, bf16[64,8,1024]{0,1,2:T(8,128)(2,1)}, u32[]{:S(2)}) copy-start(bf16[64,8,1024]{0,1,2:T(8,128)(2,1)} %get-tuple-element.26) | copy-start | bytes 3145732
  55.5 9.0 %copy-start.5 = (bf16[64,8,1024]{2,1,0:T(8,128)(2,1)S(1)}, bf16[64,8,1024]{2,1,0:T(8,128)(2,1)}, u32[]{:S(2)}) copy-start(bf16[64,8,1024]{2,1,0:T(8,128)(2,1)} %copy.34) | copy-start | bytes 3145732
  55.5 10.0 %copy-start.4 = (bf16[64,8,1024]{2,1,0:T(8,128)(2,1)S(1)}, bf16[64,8,1024]{2,1,0:T(8,128)(2,1)}, u32[]{:S(2)}) copy-start(bf16[64,8,1024]{2,1,0:T(8,128)(2,1)} %copy.31) | copy-start | bytes 3145732
  55.5 10.9 %copy-start.3 = (bf16[64,8,1024]{2,1,0:T(8,128)(2,1)S(1)}, bf16[64,8,1024]{2,1,0:T(8,128)(2,1)}, u32[]{:S(2)}) copy-start(bf16[64,8,1024]{2,1,0:T(8,128)(2,1)} %copy.28) | copy-start | bytes 3145732
  68.8 6.5 %collective-permute-start.1 = (bf16[64,7]{1,0:T(8,128)(2,1)S(1)}, bf16[64,7]{1,0:T(8,128)(2,1)S(1)}, u32[]{:S(2)}, u32[]{:S(2)}) collective-permute-start(bf16[64,7]{1,0:T(8,128)(2,1)S(1)} %slice.369), channel_id=1, source_target_pairs={{2,0},{4,2},{6,4},{8,6},{10,8},{12,10},{14,12},{16,14},{18,16},{20... | collective-permute-start | bytes 2696 | tf_op jit(solution)/shard_map/ppermute | solution.py:14
  242.0 1.9 copy-start
  270.1 26.8 %copy-start.6 = (f32[896,128]{1,0:T(8,128)S(1)}, f32[896,128]{1,0:T(8,128)}, u32[]{:S(2)}) copy-start(f32[896,128]{1,0:T(8,128)} %convolution_subtract_fusion) | copy-start | bytes 1376260
  578.7 1.0 copy-start.7
Sparse Core Ops, SparseCore 0:
  81.8 145.2 all-reduce.2
where the time goes:
time: 596 us; the launch traced here: 587 us
  other arithmetic  268 us (45%)
  waiting for transfers between devices  154 us (26%)
  local copies, waits for them, and re-layouts  84.7 us (14%)
  matrix products  54.8 us (9%)
  between operations  19.8 us (3%)
    another operation x30, other arithmetic, local(): lower_factor = jnp.linalg.cholesky(covariance)  173 us
    psum x1, waiting for transfers between devices, local(): gram_full = lax.psum(inner_gram(hankel, hankel), ('tm', 'chan'))  145 us
    another operation x3, other arithmetic, local(): jax.scipy.linalg.solve_triangular(lower_factor, hankel.astype(jnp.float32...  84.4 us
    slice x9, local copies, waits for them, and re-layouts, decimate(): window = phases[:, :, j:j + out_rows]  37.8 us
    another operation x24, local copies, waits for them, and re-layouts  27.7 us
    another operation x14, matrix products, local(): lower_factor = jnp.linalg.cholesky(covariance)  23.5 us
    another operation x15, matrix products, local(): jax.scipy.linalg.solve_triangular(lower_factor, hankel.astype(jnp.float32...  15.2 us
    dot_general x8, matrix products, decimate(): jnp.einsum('csn,cs->cn', window, weights, precision=lax.Precision.HIGHEST)  12.8 us
  transfers between devices with their start and end apart: 3, of which 3 were waited for; matrix products, arithmetic and copies ran while one was open for 0% of the time, Pallas kernels for 0%

commit v1 on v0

--- a/solution.py
+++ b/solution.py
@@ -48,7 +48,9 @@
     window = lax.dynamic_slice_in_dim(gathered, first_col, row_count + LAGS - 1, 1)
     hankel = jnp.concatenate([window[:, i : i + row_count] for i in range(LAGS)], axis=0)
     columns = hankel.shape[0]
-    gram_full = lax.psum(inner_gram(hankel, hankel), ("tm", "chan"))
+    gram_full = inner_gram(hankel, hankel)
+    for mesh_axis in ("chan", "tm"):
+        gram_full = lax.psum(gram_full, mesh_axis)
     devices_all = lax.axis_size(("tm", "chan"))
     covariance = gram_full / (row_count * devices_all)
     lower_factor = jnp.linalg.cholesky(covariance)

time: 596 us -> 658 us (1.10)
  waiting for transfers between devices: 154 us -> 217 us
    psum x1 -> x2, waiting for transfers between devices: 145 us -> 208 us  [local(): gram_full = lax.psum(gram_full, mesh_axis)]
  transfers between devices with their start and end apart: 3 -> 4, of which waited for: 3 -> 4; matrix products, arithmetic and copies ran while one was open for 0% -> 0% of each run, Pallas kernels for 0% -> 0%
where the time goes in v1:
time: 658 us; the launch traced here: 649 us
  other arithmetic  268 us (41%)
  waiting for transfers between devices  217 us (33%)
  local copies, waits for them, and re-layouts  84.7 us (13%)
  matrix products  54.8 us (8%)
  between operations  19.8 us (3%)
    psum x2, waiting for transfers between devices, local(): gram_full = lax.psum(gram_full, mesh_axis)  208 us
    another operation x30, other arithmetic, local(): lower_factor = jnp.linalg.cholesky(covariance)  173 us
    another operation x3, other arithmetic, local(): jax.scipy.linalg.solve_triangular(lower_factor, hankel.astype(jnp.float32...  84.4 us
    slice x9, local copies, waits for them, and re-layouts, decimate(): window = phases[:, :, j:j + out_rows]  37.8 us
    another operation x24, local copies, waits for them, and re-layouts  27.7 us
    another operation x14, matrix products, local(): lower_factor = jnp.linalg.cholesky(covariance)  23.5 us
    another operation x15, matrix products, local(): jax.scipy.linalg.solve_triangular(lower_factor, hankel.astype(jnp.float32...  15.2 us
  transfers between devices with their start and end apart: 4, of which 4 were waited for; matrix products, arithmetic and copies ran while one was open for 0% of the time, Pallas kernels for 0%

profile of v1, /device:TPU:0, one launch (start us, length us, event | category | flops | bytes accessed | tf_op | source)
XLA Modules:
  0.0 649.3 jit_solution(8270675653038545018)
XLA Ops:
  10.4 4.1 collective-permute-done
  17.6 5.9 fusion.66
  23.5 4.4 copy.46
  27.9 4.3 copy.43
  32.1 4.3 copy.40
  36.4 3.3 copy.37
  39.8 4.4 copy.34
  44.2 4.3 copy.31
  48.5 4.3 copy.28
  52.8 2.7 copy.25
  55.5 2.3 fusion.75
  70.1 5.2 collective-permute-done.1
  78.4 3.2 fusion.76
  81.6 32.0 %all-reduce.4.cloned.1.call-done = f32[1024,1024]{0,1:T(8,128)} async-done(((f32[1024,1024]{0,1:T(8,128)}), f32[1024,1024]{0,1:T(8,128)}) %all-reduce.4.cloned.1.call-update) | async-done | bytes 4194320 | tf_op jit(solution)/shard_map/psum | solution.py:53
  114.0 175.6 %all-reduce.6.cloned.1.call-done = f32[1024,1024]{0,1:T(8,128)} async-done(((f32[1024,1024]{0,1:T(8,128)}), f32[1024,1024]{0,1:T(8,128)}) %all-reduce.6.cloned.1.call-update) | async-done | bytes 4194320 | tf_op jit(solution)/shard_map/psum | solution.py:53
  289.5 5.0 broadcast_multiply_fusion
  294.5 5.5 copy.16
  300.1 4.4 fusion
  306.5 11.7 %cholesky.223 = f32[128,128]{1,0:T(8,128)S(1)} custom-call(f32[128,128]{1,0:T(8,128)S(1)} %cholesky.580), custom_call_target="Cholesky" | custom-call | tf_op jit(solution)/shard_map/jit(cholesky)/cholesky | solution.py:56
  318.2 9.8 %custom-call.63 = f32[1,128,128]{1,2,0:T(8,128)S(1)} custom-call(f32[1,128,128]{2,1,0:T(8,128)S(1)} %get-tuple-element.72), custom_call_target="InvertDiagBlocksLowerTriangular" | custom-call | tf_op jit(solution)/shard_map/jit(cholesky)/cholesky | solution.py:56
  329.7 2.7 convolution_subtract_fusion
  333.6 12.1 %cholesky.244 = f32[128,128]{1,0:T(8,128)S(1)} custom-call(f32[128,128]{1,0:T(8,128)S(1)} %cholesky.584), custom_call_target="Cholesky" | custom-call | tf_op jit(solution)/shard_map/jit(cholesky)/cholesky | solution.py:56
  345.6 2.5 cholesky.255
  349.7 9.8 %custom-call.64 = f32[1,128,128]{1,2,0:T(8,128)S(1)} custom-call(f32[1,128,128]{2,1,0:T(8,128)S(1)} %get-tuple-element.69), custom_call_target="InvertDiagBlocksLowerTriangular" | custom-call | tf_op jit(solution)/shard_map/jit(cholesky)/cholesky | solution.py:56
  362.8 11.7 %cholesky.468 = f32[128,128]{1,0:T(8,128)S(1)} custom-call(f32[128,128]{1,0:T(8,128)S(1)} %cholesky.589), custom_call_target="Cholesky" | custom-call | tf_op jit(solution)/shard_map/jit(cholesky)/cholesky | solution.py:56
  375.2 9.8 %custom-call.65 = f32[1,128,128]{1,2,0:T(8,128)S(1)} custom-call(f32[1,128,128]{2,1,0:T(8,128)S(1)} %get-tuple-element.66), custom_call_target="InvertDiagBlocksLowerTriangular" | custom-call | tf_op jit(solution)/shard_map/jit(cholesky)/cholesky | solution.py:56
  386.2 2.3 convolution_subtract_fusion.2
  388.5 11.9 %cholesky.487 = f32[128,128]{1,0:T(8,128)S(1)} custom-call(f32[128,128]{1,0:T(8,128)S(1)} %cholesky.594), custom_call_target="Cholesky" | custom-call | tf_op jit(solution)/shard_map/jit(cholesky)/cholesky | solution.py:56
  401.0 9.8 %custom-call.66 = f32[1,128,128]{1,2,0:T(8,128)S(1)} custom-call(f32[1,128,128]{2,1,0:T(8,128)S(1)} %get-tuple-element.63), custom_call_target="InvertDiagBlocksLowerTriangular" | custom-call | tf_op jit(solution)/shard_map/jit(cholesky)/cholesky | solution.py:56
  411.9 2.3 convolution_subtract_fusion.10
  414.3 11.7 %cholesky.506 = f32[128,128]{1,0:T(8,128)S(1)} custom-call(f32[128,128]{1,0:T(8,128)S(1)} %cholesky.599), custom_call_target="Cholesky" | custom-call | tf_op jit(solution)/shard_map/jit(cholesky)/cholesky | solution.py:56
  426.6 10.0 %custom-call.67 = f32[1,128,128]{1,2,0:T(8,128)S(1)} custom-call(f32[1,128,128]{2,1,0:T(8,128)S(1)} %get-tuple-element.60), custom_call_target="InvertDiagBlocksLowerTriangular" | custom-call | tf_op jit(solution)/shard_map/jit(cholesky)/cholesky | solution.py:56
  440.0 11.7 %cholesky.526 = f32[128,128]{1,0:T(8,128)S(1)} custom-call(f32[128,128]{1,0:T(8,128)S(1)} %cholesky.604), custom_call_target="Cholesky" | custom-call | tf_op jit(solution)/shard_map/jit(cholesky)/cholesky | solution.py:56
  452.3 9.8 %custom-call.68 = f32[1,128,128]{1,2,0:T(8,128)S(1)} custom-call(f32[1,128,128]{2,1,0:T(8,128)S(1)} %get-tuple-element.57), custom_call_target="InvertDiagBlocksLowerTriangular" | custom-call | tf_op jit(solution)/shard_map/jit(cholesky)/cholesky | solution.py:56
  465.1 12.1 %cholesky.546 = f32[128,128]{1,0:T(8,128)S(1)} custom-call(f32[128,128]{1,0:T(8,128)S(1)} %cholesky.609), custom_call_target="Cholesky" | custom-call | tf_op jit(solution)/shard_map/jit(cholesky)/cholesky | solution.py:56
  477.9 9.8 %custom-call.69 = f32[1,128,128]{1,2,0:T(8,128)S(1)} custom-call(f32[1,128,128]{2,1,0:T(8,128)S(1)} %get-tuple-element.54), custom_call_target="InvertDiagBlocksLowerTriangular" | custom-call | tf_op jit(solution)/shard_map/jit(cholesky)/cholesky | solution.py:56
  490.3 11.7 %cholesky.564 = f32[128,128]{1,0:T(8,128)S(1)} custom-call(f32[128,128]{1,0:T(8,128)S(1)} %convolution_subtract_fusion.13), custom_call_target="Cholesky" | custom-call | tf_op jit(solution)/shard_map/jit(cholesky)/cholesky | solution.py:56
  512.2 4.8 fusion.1
  518.1 27.7 %while.1 = (s32[]{:T(128)}, f32[1024,1024]{1,0:T(8,128)}, s32[8,2]{0,1:T(2,128)S(1)}, f32[8,128,128]{2,1,0:T(8,128)}, s32[]{:T(128)}) while((s32[]{:T(128)}, f32[1024,1024]{1,0:T(8,128)}, s32[8,2]{0,1:T(2,128)S(1)}, f32[8,128,128]{2,1,0:T(8,128)}, s32[]{:T(128)}) %tuple.73), condition=%wide.while_cond, body=%wide.while_body.sunk | while | flops 2 | bytes 132205 | solution.py:60
  518.7 2.9 bitcast_dynamic-update-slice_fusion.2
  522.2 2.9 bitcast_dynamic-update-slice_fusion.2
  525.6 2.9 bitcast_dynamic-update-slice_fusion.2
  529.1 2.9 bitcast_dynamic-update-slice_fusion.2
  532.6 2.9 bitcast_dynamic-update-slice_fusion.2
  536.1 2.9 bitcast_dynamic-update-slice_fusion.2
  539.5 2.9 bitcast_dynamic-update-slice_fusion.2
  543.0 2.8 bitcast_dynamic-update-slice_fusion.2
  545.8 79.6 %custom-call.70 = f32[8,128,128]{1,2,0:T(8,128)S(1)} custom-call(f32[8,128,128]{2,1,0:T(8,128)} %get-tuple-element.9), custom_call_target="InvertDiagBlocksLowerTriangular" | custom-call | tf_op jit(solution)/shard_map/jit(_solve_triangular)/triangular_solve | solution.py:60
  (124 shorter events, 73.7 us)
Async XLA Ops:
  7.2 106.5 %all-reduce.4.cloned.1.call-start = ((), (), s32[]{:S(2)}) async-start(), calls=%async_computation | async-start | bytes 8388608 | tf_op jit(solution)/shard_map/psum | solution.py:53
  7.9 6.5 %collective-permute-start = (bf16[64,56]{1,0:T(8,128)(2,1)S(1)}, bf16[64,56]{1,0:T(8,128)(2,1)S(1)}, u32[]{:S(2)}, u32[]{:S(2)}) collective-permute-start(bf16[64,56]{1,0:T(8,128)(2,1)S(1)} %slice.324), channel_id=1, source_target_pairs={{2,0},{4,2},{6,4},{8,6},{10,8},{12,10},{14,12},{16,14},{18,16},{20... | collective-permute-start | bytes 21512 | tf_op jit(solution)/shard_map/ppermute | solution.py:14
  23.5 12.9 %copy-start.2 = (bf16[64,8,1024]{0,1,2:T(8,128)(2,1)S(1)}, bf16[64,8,1024]{0,1,2:T(8,128)(2,1)}, u32[]{:S(2)}) copy-start(bf16[64,8,1024]{0,1,2:T(8,128)(2,1)} %get-tuple-element.30) | copy-start | bytes 3145732
  39.8 13.0 %copy-start.1 = (bf16[64,8,1024]{0,1,2:T(8,128)(2,1)S(1)}, bf16[64,8,1024]{0,1,2:T(8,128)(2,1)}, u32[]{:S(2)}) copy-start(bf16[64,8,1024]{0,1,2:T(8,128)(2,1)} %get-tuple-element.26) | copy-start | bytes 3145732
  55.5 9.0 %copy-start.5 = (bf16[64,8,1024]{2,1,0:T(8,128)(2,1)S(1)}, bf16[64,8,1024]{2,1,0:T(8,128)(2,1)}, u32[]{:S(2)}) copy-start(bf16[64,8,1024]{2,1,0:T(8,128)(2,1)} %copy.34) | copy-start | bytes 3145732
  55.5 10.0 %copy-start.4 = (bf16[64,8,1024]{2,1,0:T(8,128)(2,1)S(1)}, bf16[64,8,1024]{2,1,0:T(8,128)(2,1)}, u32[]{:S(2)}) copy-start(bf16[64,8,1024]{2,1,0:T(8,128)(2,1)} %copy.31) | copy-start | bytes 3145732
  55.5 10.9 %copy-start.3 = (bf16[64,8,1024]{2,1,0:T(8,128)(2,1)S(1)}, bf16[64,8,1024]{2,1,0:T(8,128)(2,1)}, u32[]{:S(2)}) copy-start(bf16[64,8,1024]{2,1,0:T(8,128)(2,1)} %copy.28) | copy-start | bytes 3145732
  68.8 6.5 %collective-permute-start.1 = (bf16[64,7]{1,0:T(8,128)(2,1)S(1)}, bf16[64,7]{1,0:T(8,128)(2,1)S(1)}, u32[]{:S(2)}, u32[]{:S(2)}) collective-permute-start(bf16[64,7]{1,0:T(8,128)(2,1)S(1)} %slice.369), channel_id=1, source_target_pairs={{2,0},{4,2},{6,4},{8,6},{10,8},{12,10},{14,12},{16,14},{18,16},{20... | collective-permute-start | bytes 2696 | tf_op jit(solution)/shard_map/ppermute | solution.py:14
  81.6 207.9 %all-reduce.6.cloned.1.call-start = ((), (), s32[]{:S(2)}) async-start(), calls=%async_computation.1 | async-start | bytes 8388608 | tf_op jit(solution)/shard_map/psum | solution.py:53
  304.5 1.9 copy-start
  332.6 26.8 %copy-start.6 = (f32[896,128]{1,0:T(8,128)S(1)}, f32[896,128]{1,0:T(8,128)}, u32[]{:S(2)}) copy-start(f32[896,128]{1,0:T(8,128)} %convolution_subtract_fusion) | copy-start | bytes 1376260
  641.3 1.0 copy-start.7
Sparse Core Ops, SparseCore 0:
  81.7 31.8 all-reduce.3
  120.2 169.2 all-reduce.5
